TPU v7x, 512 devices: a whole 4x8x8 slice. The times are simulated.
512 devices in a mesh: dp: 64 (over z_lo, x, y), feat: 8 (over z_hi, core).
Axes of the slice: x: 4, y: 8, z: 8 (z_hi: 4, z_lo: 2; z = z_hi * 2 + z_lo), core: 2. Of those that a mesh axis runs over, the one named last changes fastest.
Arguments:
- data: bfloat16 [32768, 28672], P('dp', 'feat'), may hold values from -100 to 100
- basis: float32 [8, 3584, 256], P('feat', 'dp'), may hold values from -6 to 6
Outputs:
- new_basis: float32 [8, 3584, 256], P('feat', 'dp')
All inputs are finite; a program needn't handle non-finite values.
Results may differ from a plain program's by a relative error of at most 0.011.
Values may be sent and summed in bfloat16 or wider, within the bound.
A program may use at most 64 MiB of HBM per device.

v0:
```python
import jax
import jax.numpy as jnp
from jax import lax
from jax.sharding import PartitionSpec as P

F = 28672


def per_device(data, basis):
    row_count = data.shape[0]
    owned = basis.shape[1]
    width = basis.shape[2]
    rounded = basis.astype(jnp.bfloat16)
    whole = lax.all_gather(rounded, "dp", axis=1, tiled=True)
    partial_y = jnp.dot(data, whole[0], preferred_element_type=jnp.float32)
    summed = lax.psum(partial_y.astype(jnp.bfloat16), "feat")
    token_total = float(row_count * lax.axis_size("dp"))
    product = lax.psum_scatter(
        lax.dot_general(data, summed, (((0,), (0,)), ((), ())), preferred_element_type=jnp.float32),
        "dp",
        scatter_dimension=0,
        tiled=True,
    )
    product = product / token_total
    local_gram = jnp.dot(
        product.T, product, precision=lax.Precision.HIGHEST, preferred_element_type=jnp.float32
    )
    gram = lax.psum(local_gram, ("dp", "feat"))
    gram = gram / float(F)
    lower = jnp.linalg.cholesky(gram)
    result = lax.linalg.triangular_solve(
        lower, product, left_side=False, lower=True, transpose_a=True
    )
    return result.reshape(1, owned, width)


def solution(mesh):
    in_specs = (P("dp", "feat"), P("feat", "dp", None))
    out_specs = P("feat", "dp", None)
    return jax.shard_map(
        per_device, mesh=mesh, in_specs=in_specs, out_specs=out_specs, check_vma=False
    )
```

profile of v0, /device:TPU:1, one launch (start us, length us, event | category | flops | bytes accessed | tf_op | source)
XLA Modules:
  0.0 1066.2 jit_solution(6394573011791259125)
XLA Ops:
  6.5 0.0 all-gather.2.cloned.1.call-start
  6.5 1.4 convert_element_type.6
  8.0 0.0 all-gather.2.cloned.1.call-update
  8.0 0.0 all-reduce.4.cloned.1.call-start
  8.0 265.1 %all-gather.2.cloned.1.call-done = bf16[1,3584,256]{2,1,0:T(8,128)(2,1)} async-done(((bf16[1,56,256]{2,1,0:T(8,128)(2,1)}), bf16[1,3584,256]{2,1,0:T(8,128)(2,1)}) %all-gather.2.cloned.1.call-update) | async-done | bytes 1835024 | tf_op jit(solution)/shard_map/all_gather | solution.py:14
  273.1 4.4 fusion.2
  277.5 0.0 all-reduce.4.cloned.1.call-update
  277.6 0.0 reduce-scatter.4.cloned.1.call-start
  277.6 119.2 %all-reduce.4.cloned.1.call-done = bf16[512,256]{1,0:T(8,128)(2,1)} async-done(((bf16[512,256]{1,0:T(8,128)(2,1)}), bf16[512,256]{1,0:T(8,128)(2,1)}) %all-reduce.4.cloned.1.call-update) | async-done | bytes 262160 | tf_op jit(solution)/shard_map/psum | solution.py:16
  396.8 5.1 convolution_bitcast_fusion
  401.8 5.1 copy.8
  407.0 0.0 reduce-scatter.4.cloned.1.call-update
  407.0 0.2 all-reduce.6.cloned.1.call-start
  407.3 274.7 %reduce-scatter.4.cloned.1.call-done = f32[56,256]{1,0:T(8,128)} async-done(((f32[3584,256]{1,0:T(8,128)}), f32[56,256]{1,0:T(8,128)}) %reduce-scatter.4.cloned.1.call-update) | async-done | bytes 57360
  682.0 0.9 copy.9
  682.9 1.1 fusion.13
  684.0 0.0 all-reduce.6.cloned.1.call-update
  684.1 312.2 %all-reduce.6.cloned.1.call-done = f32[256,256]{0,1:T(8,128)} async-done(((f32[256,256]{0,1:T(8,128)}), f32[256,256]{0,1:T(8,128)}) %all-reduce.6.cloned.1.call-update) | async-done | bytes 262160 | tf_op jit(solution)/shard_map/psum | solution.py:28
  996.3 1.0 broadcast_multiply_fusion
  997.3 0.1 copy.6
  997.4 1.0 fusion.5
  998.4 11.7 %cholesky.50 = f32[128,128]{1,0:T(8,128)S(1)} custom-call(f32[128,128]{1,0:T(8,128)S(1)} %cholesky.118), custom_call_target="Cholesky" | custom-call | tf_op jit(solution)/shard_map/jit(cholesky)/cholesky | solution.py:30
  1010.2 9.8 custom-call.14
  1020.0 0.2 constant_dynamic-update-slice_fusion.1
  1020.2 0.3 convolution_subtract_fusion.1
  1020.5 11.7 %cholesky.105 = f32[128,128]{1,0:T(8,128)S(1)} custom-call(f32[128,128]{1,0:T(8,128)S(1)} %convolution_subtract_fusion.1), custom_call_target="Cholesky" | custom-call | tf_op jit(solution)/shard_map/jit(cholesky)/cholesky | solution.py:30
  1032.2 0.7 compare_reduce_fusion
  1034.2 0.1 triangular_solve.58
  1034.3 4.2 while.1
  1034.5 0.7 fusion.23
  1035.2 1.3 bitcast_dynamic-update-slice_fusion.2
  1036.5 0.7 fusion.23
  1037.2 1.3 bitcast_dynamic-update-slice_fusion.2
  1038.6 19.7 %custom-call.15 = f32[2,128,128]{1,2,0:T(8,128)S(1)} custom-call(f32[2,128,128]{2,1,0:T(8,128)S(1)} %get-tuple-element.12), custom_call_target="InvertDiagBlocksLowerTriangular" | custom-call | tf_op jit(solution)/shard_map/triangular_solve | solution.py:31
  1058.2 0.3 fusion.8
  1058.5 0.2 convolution_subtract_fusion
  1058.7 0.3 fusion.6
  1059.0 0.6 maximum_bitcast_fusion
  (10 shorter events, 0.2 us)
Async XLA Ops:
  6.5 266.6 %all-gather.2.cloned.1.call-start = ((), (), s32[]{:S(2)}) async-start(), calls=%async_computation.1 | async-start | bytes 1863680 | tf_op jit(solution)/shard_map/all_gather | solution.py:14
  8.0 388.8 %all-reduce.4.cloned.1.call-start = ((), (), s32[]{:S(2)}) async-start(), calls=%async_computation.2 | async-start | bytes 524288 | tf_op jit(solution)/shard_map/psum | solution.py:16
  277.6 404.4 %reduce-scatter.4.cloned.1.call-start = ((), (), s32[]{:S(2)}) async-start(), calls=%async_computation.4 | async-start | bytes 3727360
  407.0 589.3 %all-reduce.6.cloned.1.call-start = ((), (), s32[]{:S(2)}) async-start(), calls=%async_computation.3 | async-start | bytes 524288 | tf_op jit(solution)/shard_map/psum | solution.py:28
Sparse Core Ops, SparseCore 0:
  9.4 263.6 all-gather.1
  277.7 119.0 all-reduce.3
  407.1 274.8 reduce-scatter.3
  686.8 309.3 all-reduce.5
where the time goes:
time: 1070 us
  waiting for transfers between devices  971 us (91%)
  other arithmetic  57.8 us (5%)
  between operations  14.5 us (1%)
  matrix products  11.8 us (1%)
    psum x1, waiting for transfers between devices, per_device(): gram = lax.psum(local_gram, ('dp', 'feat'))  312 us
    unnamed x5, waiting for transfers between devices  275 us
    all_gather x1, waiting for transfers between devices, per_device(): whole = lax.all_gather(rounded, 'dp', axis=1, tiled=True)  265 us
    psum x1, waiting for transfers between devices, per_device(): summed = lax.psum(partial_y.astype(jnp.bfloat16), 'feat')  119 us
    another operation x6, other arithmetic, per_device(): lower = jnp.linalg.cholesky(gram)  34 us
  transfers between devices with their start and end apart: 4, of which 4 were waited for; matrix products, arithmetic and copies ran while one was open for 0% of the time, Pallas kernels for 0%

commit v1 on v0

v1 whole, which is shorter than its diff:
```python
import jax
import jax.numpy as jnp
from jax import lax
from jax.experimental import pallas as pl
from jax.experimental.pallas import tpu as pltpu
from jax.sharding import PartitionSpec as P

F32 = jnp.float32
BF16 = jnp.bfloat16
MESH = pl.DeviceIdType.MESH
HI = lax.Precision.HIGHEST


class Cfg:
    def __init__(self, zl, x, y, zh, core, tokens, own=56, width=256, chunks=1):
        self.ZL, self.X, self.Y, self.ZH, self.C = zl, x, y, zh, core
        self.T, self.OWN, self.K, self.NC = tokens, own, width, chunks
        self.Z = zl * zh
        self.FE = zh * core
        self.DP = zl * x * y
        self.FS = own * self.DP
        self.CW = width // chunks
        self.TOTAL_T = tokens * self.DP
        self.F = self.FS * self.FE
        self.MX = x * core
        self.RX = width // self.MX
        self.RZ = self.RX * 2 // self.Z


ALPHA = 64


def reach(n, direction, sign):
    return n // 2 if direction == sign else n // 2 - 1


def offsets(n, sign):
    out = [0]
    for d in (1, -1):
        out += [d * h for h in range(1, reach(n, d, sign) + 1)]
    return out


def sgn(h):
    return (h > 0) - (h < 0)


class Part:
    def __init__(self, cfg, index):
        self.index = index
        self.sign = 1 if index == 0 else -1
        self.axes = ("y", "x") if index == 0 else ("x", "y")
        size = {"x": cfg.X, "y": cfg.Y}
        self.n = tuple(size[a] for a in self.axes)
        self.r0 = 0 if index == 0 else ALPHA
        self.rows = ALPHA if index == 0 else 2 * cfg.OWN - ALPHA
        self.events = [
            (a, b) for a in offsets(self.n[0], self.sign) for b in offsets(self.n[1], self.sign)
        ]
        self.id = {e: i for i, e in enumerate(self.events)}

    def can(self, axis, h, direction):
        return (h == 0 or sgn(h) == direction) and abs(h) + 1 <= reach(
            self.n[axis], direction, self.sign
        )


def comm_kernel(cfg, basis_ref, data_hbm, z_ref, gram_ref,
                xb, zs, zr, g, q, ypart, yr, yfull, zp, stage, rs, fin, zx_s, zx_r,
                g1, r1, s1, r2, s2, r3, s3, a2, gfull,
                xsem, zsem, ag_send, ag_recv, y_sem, rs_send, rs_recv, zx_sem,
                m1, m2, m3, m4, m5):
    X, Y, Z, ZL, C, NC, CW = cfg.X, cfg.Y, cfg.Z, cfg.ZL, cfg.C, cfg.NC, cfg.CW
    OWN = cfg.OWN
    dp = lax.axis_index("dp")
    feat = lax.axis_index("feat")
    my = dp % Y
    mx = (dp // Y) % X
    zl = dp // (X * Y)
    mc = feat % C
    mz = (feat // C) * ZL + zl
    me = {"x": mx, "y": my}

    def dev(ox=0, oy=0, oz=0, oc=0):
        x = (mx + ox + X) % X
        y = (my + oy + Y) % Y
        z = (mz + oz + Z) % Z
        c = (mc + oc) % C
        return {"dp": ((z % ZL) * X + x) * Y + y, "feat": (z // ZL) * C + c}

    partner = dev(oz=1 - 2 * zl)

    def rdma(src, dst, ssem, rsem, device):
        return pltpu.make_async_remote_copy(
            src_ref=src, dst_ref=dst, send_sem=ssem, recv_sem=rsem,
            device_id=device, device_id_type=MESH,
        )

    load = pltpu.make_async_copy(data_hbm, xb, xsem)
    load.start()

    own = basis_ref[0].astype(BF16).astype(F32)
    zs[...] = jnp.concatenate([own, jnp.zeros((64 - OWN, cfg.K), F32)], axis=0).astype(BF16)

    xc = [(ox, oc) for ox in range(X) for oc in range(C) if (ox, oc) != (0, 0)]
    fe = [(oz, oc) for oz in range(0, Z, ZL) for oc in range(C) if (oz, oc) != (0, 0)]
    peers = {(ox, 0, 0, oc) for ox, oc in xc}
    peers |= {(0, oy, 0, 0) for oy in range(1, Y)}
    peers |= {(0, 0, oz, 0) for oz in range(1, Z)}
    peers |= {(0, 0, oz, oc) for oz, oc in fe}
    barrier = pltpu.get_barrier_semaphore()
    for peer in sorted(peers):
        pl.semaphore_signal(barrier, inc=1, device_id=dev(*peer), device_id_type=MESH)
    pl.semaphore_wait(barrier, len(peers))

    swap = rdma(zs, zr, zsem.at[0], zsem.at[1], partner)
    swap.start()
    swap.wait_recv()
    other = zr[...].astype(F32)[:OWN]
    unit = jnp.concatenate(
        [jnp.where(zl == 0, own, other), jnp.where(zl == 0, other, own)], axis=0
    ).astype(BF16)
    for c in range(NC):
        g[c, mx, my] = unit[:, c * CW:(c + 1) * CW]

    parts = [Part(cfg, 0), Part(cfg, 1)]
    pending = [swap]

    def near(axis, direction):
        return dev(ox=direction) if axis == "x" else dev(oy=direction)

    def origin(part, e):
        at = {}
        for k in range(2):
            n = part.n[k]
            at[part.axes[k]] = (me[part.axes[k]] - e[k] + n) % n
        return at["x"], at["y"]

    def gather(c):
        todo = [(abs(e[0]) + abs(e[1]), p.index, p.id[e], p, e) for p in parts for e in p.events]
        todo.sort(key=lambda t: t[:3])
        count = [0, 0]
        for _, pi, ei, p, e in todo:
            ux, uy = origin(p, e)
            slot = g.at[c, ux, uy, pl.ds(p.r0, p.rows)]
            if e != (0, 0):
                rdma(slot, slot, ag_send.at[c, pi, 0], ag_recv.at[c, pi, ei], partner).wait_recv()
            for k in range(2):
                if k == 0 and e[1] != 0:
                    continue
                for d in (1, -1):
                    if not p.can(k, e[k], d):
                        continue
                    to = (e[0] + d, e[1]) if k == 0 else (e[0], e[1] + d)
                    cp = rdma(slot, slot, ag_send.at[c, pi, count[pi]],
                              ag_recv.at[c, pi, p.id[to]], near(p.axes[k], d))
                    count[pi] += 1
                    cp.start()
                    pending.append(cp)

    def arrange(c):
        def pair(i, carry):
            ux = i // (Y // 2)
            uy = (i % (Y // 2)) * 2
            a = g[c, ux, uy].astype(F32)
            b = g[c, ux, uy + 1].astype(F32)
            for zz in range(ZL):
                rows = jnp.concatenate(
                    [a[zz * OWN:(zz + 1) * OWN], b[zz * OWN:(zz + 1) * OWN]], axis=0
                ).astype(BF16)
                at = pl.multiple_of(((zz * X + ux) * Y + uy) * OWN, 2 * OWN)
                q[c, pl.ds(at, 2 * OWN)] = rows
            return carry
        lax.fori_loop(0, X * Y // 2, pair, 0)

    TS = cfg.T // cfg.FE

    def sum_y(c):
        part = jnp.dot(xb[...], q[c], preferred_element_type=F32).astype(BF16)
        for k in range(cfg.FE):
            ypart[c, k] = part[k * TS:(k + 1) * TS]
        copies = []
        for i, (oz, oc) in enumerate(fe):
            to = dev(oz=oz, oc=oc)
            cp = rdma(ypart.at[c, to["feat"]], yr.at[c, i], y_sem.at[c, 0, i], y_sem.at[c, 1, i], to)
            cp.start()
            copies.append(cp)
        total = ypart[c, feat].astype(F32)
        for i, cp in enumerate(copies):
            cp.wait_recv()
            total = total + yr[c, i].astype(F32)
        yfull[c, feat] = total.astype(BF16)
        pending.extend(copies)
        copies = []
        for i, (oz, oc) in enumerate(fe):
            cp = rdma(yfull.at[c, feat], yfull.at[c, feat], y_sem.at[c, 2, i], y_sem.at[c, 3, i],
                      dev(oz=oz, oc=oc))
            cp.start()
            copies.append(cp)
        for i, (oz, oc) in enumerate(fe):
            frm = dev(oz=-oz, oc=oc)["feat"]
            rdma(yfull.at[c, frm], yfull.at[c, frm], y_sem.at[c, 2, i], y_sem.at[c, 3, i],
                 dev(oz=oz, oc=oc)).wait_recv()
        pending.extend(copies)

    def product(c):
        y = yfull[c].reshape(cfg.T, CW)
        zp[c] = lax.dot_general(xb[...], y, (((0,), (0,)), ((), ())), preferred_element_type=F32)

    def scatter(c):
        todo = [(-abs(e[0]) - abs(e[1]), p.index, p.id[e], p, e) for p in parts for e in p.events]
        todo.sort(key=lambda t: t[:3])
        for _, pi, ei, p, e in todo:
            ux, uy = origin(p, e)
            at0 = pl.multiple_of((ux * Y + uy) * OWN, OWN)
            at1 = pl.multiple_of((X * Y + ux * Y + uy) * OWN, OWN)
            if pi == 0:
                v = jnp.concatenate(
                    [zp[c, pl.ds(at0, OWN)], zp[c, pl.ds(at1, ALPHA - OWN)]], axis=0
                )
            else:
                v = zp[c, pl.ds(at1 + (ALPHA - OWN), p.rows)]
            arrivals = []
            for d in (1, -1):
                if p.can(1, e[1], d):
                    arrivals.append((e[0], e[1] + d))
                if e[1] == 0 and p.can(0, e[0], d):
                    arrivals.append((e[0] + d, 0))
            for a in arrivals:
                slot = rs.at[c, pi, p.id[a], pl.ds(0, p.rows)]
                rdma(slot, slot, rs_send.at[c, pi, 0], rs_recv.at[c, pi, p.id[a]], partner).wait_recv()
                v = v + slot[...].astype(F32)
            if e == (0, 0):
                fin[c, pl.ds(p.r0, p.rows)] = v
                continue
            k = 1 if e[1] != 0 else 0
            stage[c, pi, ei, pl.ds(0, p.rows)] = v.astype(BF16)
            cp = rdma(stage.at[c, pi, ei, pl.ds(0, p.rows)], rs.at[c, pi, ei, pl.ds(0, p.rows)],
                      rs_send.at[c, pi, ei], rs_recv.at[c, pi, ei], near(p.axes[k], -sgn(e[k])))
            cp.start()
            pending.append(cp)
        lo = fin[c, pl.ds(0, OWN)]
        hi = fin[c, pl.ds(OWN, OWN)]
        zx_s[c] = jnp.where(zl == 0, hi, lo)
        cp = rdma(zx_s.at[c], zx_r.at[c], zx_sem.at[c, 0], zx_sem.at[c, 1], partner)
        cp.start()
        pending.append(cp)
        cp.wait_recv()
        return (jnp.where(zl == 0, lo, hi) + zx_r[c]) / float(cfg.TOTAL_T)

    def gram_sum(z):
        gl = lax.dot_general(z, z, (((0,), (0,)), ((), ())), precision=HI, preferred_element_type=F32)
        g1[0] = gl[:, :128]
        g1[1] = gl[:, 128:]
        RX, RZ = cfg.RX, cfg.RZ
        m = mx * C + mc

        def exchange(offs, sems, src, dst, wait):
            copies = []
            for i, off in enumerate(offs):
                cp = rdma(src(off), dst(i), sems.at[0, i], sems.at[1, i], dev(*off))
                cp.start()
                copies.append(cp)
            for i, off in enumerate(offs):
                back = wait(i, off)
                rdma(back, back, sems.at[0, i], sems.at[1, i], dev(*off)).wait_recv()
            pending.extend(copies)

        xoff = [(ox, 0, 0, oc) for ox, oc in xc]
        zoff = [(0, 0, oz, 0) for oz in range(1, Z)]
        yoff = [(0, oy, 0, 0) for oy in range(1, Y)]

        def rows1(off):
            t = ((mx + off[0] + X) % X) * C + (mc + off[3]) % C
            return pl.ds(pl.multiple_of(t * RX, RX), RX)

        mine = pl.ds(pl.multiple_of(m * RX, RX), RX)
        exchange(xoff, m1, lambda off: g1.at[:, rows1(off)], lambda i: r1.at[i], lambda i, off: r1.at[i])
        total = g1[:, mine]
        for i in range(len(xoff)):
            total = total + r1[i]
        s1[...] = total

        def tile(z):
            return z % 2, pl.ds(pl.multiple_of((z // 2) * RZ, RZ), RZ)

        def tile_to(off):
            return tile((mz + off[2] + Z) % Z)

        exchange(zoff, m2, lambda off: s1.at[tile_to(off)], lambda i: r2.at[i], lambda i, off: r2.at[i])
        half, rows = tile(mz)
        total = s1[half, rows]
        for i in range(len(zoff)):
            total = total + r2[i]
        s2[...] = total
        exchange(yoff, m3, lambda off: s2, lambda i: r3.at[i], lambda i, off: r3.at[i])
        total = s2[...]
        for i in range(len(yoff)):
            total = total + r3[i]
        a2[half, rows] = total
        own_tile = a2.at[half, rows]
        exchange(zoff, m4, lambda off: own_tile, lambda i: own_tile,
                 lambda i, off: a2.at[tile((mz - off[2] + Z) % Z)])
        gfull[:, mine] = a2[...]
        exchange(xoff, m5, lambda off: a2, lambda i: gfull.at[:, mine],
                 lambda i, off: gfull.at[:, rows1((-off[0], 0, 0, off[3]))])
        gram_ref[...] = gfull[...]

    for c in range(NC):
        gather(c)
    load.wait()
    for c in range(NC):
        arrange(c)
        sum_y(c)
        product(c)
    cols = [scatter(c) for c in range(NC)]
    z = jnp.concatenate(cols, axis=1) if NC > 1 else cols[0]
    z_ref[...] = z
    gram_sum(z)
    for cp in pending:
        cp.wait_send()


def communicate(cfg, basis, data, vmem=48 << 20):
    NC, CW, X, Y = cfg.NC, cfg.CW, cfg.X, cfg.Y
    K, OWN, T, FS = cfg.K, cfg.OWN, cfg.T, cfg.FS
    ev = X * Y
    nf, nx, nz, ny = cfg.FE - 1, cfg.MX - 1, cfg.Z - 1, Y - 1
    VM = pltpu.VMEM
    DMA = pltpu.SemaphoreType.DMA
    scratch = [
        VM((T, FS), BF16), VM((64, K), BF16), VM((64, K), BF16),
        VM((NC, X, Y, 2 * OWN, CW), BF16), VM((NC, FS, CW), BF16),
        VM((NC, cfg.FE, T // cfg.FE, CW), BF16), VM((NC, nf, T // cfg.FE, CW), BF16),
        VM((NC, cfg.FE, T // cfg.FE, CW), BF16),
        VM((NC, FS, CW), F32), VM((NC, 2, ev, ALPHA, CW), BF16), VM((NC, 2, ev, ALPHA, CW), BF16),
        VM((NC, 2 * OWN, CW), F32), VM((NC, OWN, CW), F32), VM((NC, OWN, CW), F32),
        VM((2, K, 128), F32), VM((nx, 2, cfg.RX, 128), F32), VM((2, cfg.RX, 128), F32),
        VM((nz, cfg.RZ, 128), F32), VM((cfg.RZ, 128), F32), VM((ny, cfg.RZ, 128), F32),
        VM((cfg.RZ, 128), F32), VM((2, cfg.RX, 128), F32), VM((2, K, 128), F32),
        DMA, DMA((2,)), DMA((NC, 2, ev)), DMA((NC, 2, ev)), DMA((NC, 4, nf)),
        DMA((NC, 2, ev)), DMA((NC, 2, ev)), DMA((NC, 2)),
        DMA((2, nx)), DMA((2, nz)), DMA((2, ny)), DMA((2, nz)), DMA((2, nx)),
    ]

    def body(*refs):
        comm_kernel(cfg, *refs)

    return pl.pallas_call(
        body,
        out_shape=(
            jax.ShapeDtypeStruct((OWN, K), F32),
            jax.ShapeDtypeStruct((2, K, 128), F32),
        ),
        in_specs=[pl.BlockSpec(memory_space=pltpu.VMEM), pl.BlockSpec(memory_space=pl.ANY)],
        out_specs=(pl.BlockSpec(memory_space=pltpu.VMEM), pl.BlockSpec(memory_space=pltpu.VMEM)),
        scratch_shapes=scratch,
        compiler_params=pltpu.CompilerParams(
            collective_id=0, has_side_effects=True, vmem_limit_bytes=vmem
        ),
        name="power_step",
    )(basis, data)


def split3(v):
    h = v.astype(BF16)
    r = v - h.astype(F32)
    m = r.astype(BF16)
    return h, m, (r - m.astype(F32)).astype(BF16)


def factor_kernel(scale, B, z_ref, gram_ref, out_ref, w):
    own, K = z_ref.shape
    w[:, 0:128] = gram_ref[0] * scale
    w[:, 128:256] = gram_ref[1] * scale
    w[:, 256:384] = jnp.concatenate([z_ref[...], jnp.zeros((128 - own, K), F32)], axis=0).T
    sub = lax.broadcasted_iota(jnp.int32, (8, 128), 0)
    G = B // 8
    for blk in range(K // B):
        r0 = blk * B
        t0 = r0 // 128
        tiles = list(range(t0, 3))
        v = [[w[r0 + 8 * s:r0 + 8 * s + 8, t * 128:(t + 1) * 128] for t in tiles] for s in range(G)]
        scales = []
        for s0 in range(G):
            lane = (r0 + 8 * s0) % 128
            col = {
                s: [jnp.broadcast_to(v[s][0][:, lane + k:lane + k + 1], (8, 128)) for k in range(8)]
                for s in range(s0, G)
            }
            dvec = jnp.zeros((8, 128), F32)
            for j in range(8):
                prow = [jnp.broadcast_to(v[s0][t][j:j + 1], (8, 128)) for t in range(len(tiles))]
                pcol = [jnp.broadcast_to(col[s0][k][j:j + 1], (8, 128)) if k >= j else None
                        for k in range(8)]
                inv = 1.0 / pcol[j]
                dvec = jnp.where(sub == j, pcol[j], dvec)
                for s in range(s0, G):
                    mult = col[s][j] * inv
                    if s == s0:
                        mult = jnp.where(sub > j, mult, 0.0)
                    for k in range(j + 1, 8):
                        col[s][k] = col[s][k] - mult * pcol[k]
                    for t in range(len(tiles)):
                        v[s][t] = v[s][t] - mult * prow[t]
            scales.append(lax.rsqrt(dvec))
        for s in range(G):
            for t in range(len(tiles)):
                v[s][t] = v[s][t] * scales[s]
                if tiles[t] == 2:
                    w[r0 + 8 * s:r0 + 8 * s + 8, 256:384] = v[s][t]
        if blk + 1 < K // B:
            rows = jnp.concatenate([jnp.concatenate(v[s], axis=1) for s in range(G)], axis=0)
            h, m, l = split3(rows)
            n0 = ((r0 + B) // 128) * 128 - t0 * 128
            left = jnp.concatenate([h, h, m, m, h, l], axis=0)
            right = jnp.concatenate([h, m, h, m, l, h], axis=0)
            upd = lax.dot_general(left[:, n0:K - t0 * 128], right[:, n0:], (((0,), (0,)), ((), ())),
                                  preferred_element_type=F32)
            c0 = t0 * 128 + n0
            w[r0 + B:K, c0:384] = w[r0 + B:K, c0:384] - upd[r0 + B - c0:]
    out_ref[0] = w[:, 256:384].T[:own]


def factor(cfg, z, gram, block=32):
    def body(z_ref, gram_ref, out_ref, w):
        factor_kernel(1.0 / float(cfg.F), block, z_ref, gram_ref, out_ref, w)

    return pl.pallas_call(
        body,
        out_shape=jax.ShapeDtypeStruct((1, cfg.OWN, cfg.K), F32),
        in_specs=[pl.BlockSpec(memory_space=pltpu.VMEM)] * 2,
        out_specs=pl.BlockSpec(memory_space=pltpu.VMEM),
        scratch_shapes=[pltpu.VMEM((cfg.K, 384), F32)],
        name="factor_rows",
    )(z, gram)


def solution(mesh):
    cfg = Cfg(zl=2, x=4, y=8, zh=4, core=2, tokens=512)

    def per_device(data, basis):
        z, gram = communicate(cfg, basis, data)
        return factor(cfg, z, gram)

    return jax.shard_map(
        per_device, mesh=mesh, in_specs=(P("dp", "feat"), P("feat", "dp", None)),
        out_specs=P("feat", "dp", None), check_vma=False,
    )
```

time: 1070 us -> 128 us (0.12)
  waiting for transfers between devices: 971 us -> 0 us
  Pallas kernels: 0 us -> 123 us
  other arithmetic: 57.8 us -> 0 us
  between operations: 14.5 us -> 0.02 us
  matrix products: 11.8 us -> 0 us
    psum x2 -> x0, waiting for transfers between devices: 431 us -> none  [the longest x1 312 us: per_device(): gram = lax.psum(local_gram, ('dp', 'feat'))]
    unnamed x5 -> x0, waiting for transfers between devices: 275 us -> none
    all_gather x1 -> x0, waiting for transfers between devices: 265 us -> none  [per_device(): whole = lax.all_gather(rounded, 'dp', axis=1, tiled=True)]
    pallas_call x0 -> x2, Pallas kernels: none -> 123 us  [the longest x1 114 us: communicate(): pl.pallas_call(body, out_shape=(jax.ShapeDtypeStruct((OWN, K), F32), jax....]
    another operation x9 -> x0, other arithmetic: 53.7 us -> none  [the longest x6 34 us: per_device(): lower = jnp.linalg.cholesky(gram)]
  transfers between devices with their start and end apart: 4 -> 0, of which waited for: 4 -> 0; matrix products, arithmetic and copies ran while one was open for 0% -> 0% of each run, Pallas kernels for 0% -> 0%
where the time goes in v1:
time: 128 us
  Pallas kernels  123 us (96%)
  local copies, waits for them, and re-layouts  4.15 us (3%)
    pallas_call x1, Pallas kernels, communicate(): pl.pallas_call(body, out_shape=(jax.ShapeDtypeStruct((OWN, K), F32), jax....  114 us
    pallas_call x1, Pallas kernels, factor(): pl.pallas_call(body, out_shape=jax.ShapeDtypeStruct((1, cfg.OWN, cfg.K),...  9.32 us
    unnamed x8, local copies, waits for them, and re-layouts  4.15 us

profile of v1, /device:TPU:1, one launch (start us, length us, event | category | flops | bytes accessed | tf_op | source)
XLA Modules:
  0.0 127.7 jit_solution(14552794838807985521)
XLA Ops:
  0.0 0.0 copy-start
  0.0 2.0 %copy-done = bf16[512,3584]{1,0:T(8,128)(2,1)S(1)} copy-done((bf16[512,3584]{1,0:T(8,128)(2,1)S(1)}, bf16[512,3584]{1,0:T(8,128)(2,1)}, u32[]{:S(2)}) %copy-start) | copy-done | bytes 3670040
  2.0 0.0 copy-start.2
  2.0 0.8 copy-done.2
  2.9 114.2 %power_step.1 = (f32[56,256]{1,0:T(8,128)S(1)}, f32[2,256,128]{2,1,0:T(8,128)S(1)}) custom-call(f32[1,56,256]{2,1,0:T(8,128)S(1)} %copy-done.2, bf16[512,3584]{1,0:T(8,128)(2,1)S(1)} %copy-done), custom_call_target="tpu_custom_call" | custom-call | tf_op jit(solution)/shard_map/power_step/pallas_call | solution.py:349
  117.0 0.0 copy-start.1
  117.0 0.7 copy-done.1
  117.7 0.0 copy-start.3
  117.7 0.6 copy-done.3
  118.3 9.3 %factor_rows.1 = f32[1,56,256]{2,1,0:T(8,128)} custom-call(f32[56,256]{1,0:T(8,128)} %copy-done.3, f32[2,256,128]{2,1,0:T(8,128)} %copy-done.1), custom_call_target="tpu_custom_call" | custom-call | tf_op jit(solution)/shard_map/factor_rows/pallas_call | solution.py:429
Async XLA Ops:
  0.0 2.0 %copy-start = (bf16[512,3584]{1,0:T(8,128)(2,1)S(1)}, bf16[512,3584]{1,0:T(8,128)(2,1)}, u32[]{:S(2)}) copy-start(bf16[512,3584]{1,0:T(8,128)(2,1)} %refs_1_.1) | copy-start | bytes 11010052
  2.0 0.8 copy-start.2
  117.0 0.7 copy-start.1
  117.7 0.6 copy-start.3

commit v2 on v1

v2 whole, which is shorter than its diff:
```python
import jax
import jax.numpy as jnp
from jax import lax
from jax.experimental import pallas as pl
from jax.experimental.pallas import tpu as pltpu
from jax.sharding import PartitionSpec as P

F32 = jnp.float32
BF16 = jnp.bfloat16
MESH = pl.DeviceIdType.MESH
HI = lax.Precision.HIGHEST


class Cfg:
    def __init__(self, zl, x, y, zh, core, tokens, own=56, width=256, alpha=80,
                 trees=("skip", "skip")):
        self.ZL, self.X, self.Y, self.ZH, self.C = zl, x, y, zh, core
        self.T, self.OWN, self.K = tokens, own, width
        self.Z = zl * zh
        self.FE = zh * core
        self.DP = zl * x * y
        self.FS = own * self.DP
        self.TOTAL_T = tokens * self.DP
        self.F = self.FS * self.FE
        self.MX = x * core
        self.RX = width // self.MX
        self.RZ = self.RX * 2 // self.Z
        self.alpha = alpha
        self.beta = 2 * own - alpha
        self.trees = [tree(y, kind) for kind in trees]


def tree(n, kind):
    up, down = n // 2, n // 2 - 1
    out = {}
    for h in range(1, up + 1):
        for d in ([1, -1] if h <= down else [1]):
            out[d * h] = d * (0 if kind == "direct" or h <= 2 else 2)
    return out


def position(h, n):
    s = (h + n + n // 2 - 1) % n - (n // 2 - 1)
    up = (s + n // 2 - 1) // (n // 2)
    return 2 * s * (2 * up - 1) - up


def comm_kernel(cfg, basis_ref, data_hbm, z_ref, gram_ref,
                xb, bb, zs, zr, ga, gb, q, ypart, ysib, ypair, yr, yfull, zp, sax, rax, say, ray, sby, rby, sbx, rbx, fin, zx_s, zx_r,
                g1, r1, s1, r2, s2, r3, s3, a2, gfull,
                xsem, bsem, zsem, gsem, y_sem, ssem, zx_sem,
                m1, m2, m3, m4, m5):
    X, Y, Z, ZL, ZH, C = cfg.X, cfg.Y, cfg.Z, cfg.ZL, cfg.ZH, cfg.C
    OWN, A = cfg.OWN, cfg.alpha
    dp = lax.axis_index("dp")
    feat = lax.axis_index("feat")
    my = dp % Y
    mx = (dp // Y) % X
    zl = dp // (X * Y)
    mc = feat % C
    mz = (feat // C) * ZL + zl
    me = {"x": mx, "y": my}

    def dev(ox=0, oy=0, oz=0, oc=0):
        x = (mx + ox + X) % X
        y = (my + oy + Y) % Y
        z = (mz + oz + Z) % Z
        c = (mc + oc) % C
        return {"dp": ((z % ZL) * X + x) * Y + y, "feat": (z // ZL) * C + c}

    partner = dev(oz=1 - 2 * zl)

    def rdma(src, dst, ssem, rsem, device):
        return pltpu.make_async_remote_copy(
            src_ref=src, dst_ref=dst, send_sem=ssem, recv_sem=rsem,
            device_id=device, device_id_type=MESH,
        )

    load = pltpu.make_async_copy(data_hbm, xb, xsem)
    load.start()

    fetch = pltpu.make_async_copy(basis_ref, bb, bsem)
    fetch.start()
    xc = [(ox, oc) for ox in range(X) for oc in range(C) if (ox, oc) != (0, 0)]
    fe = [(oz, oc) for oz in range(0, Z, ZL) for oc in range(C) if (oz, oc) != (0, 0)]
    peers = {(0, 0, oz, oc) for oz, oc in fe}
    peers |= {(ox, 0, 0, oc) for ox, oc in xc}
    peers |= {(0, oy, 0, 0) for oy in range(1, Y)}
    peers |= {(0, 0, oz, 0) for oz in range(1, Z)}
    barrier = pltpu.get_barrier_semaphore()
    for peer in sorted(peers):
        pl.semaphore_signal(barrier, inc=1, device_id=dev(*peer), device_id_type=MESH)
    fetch.wait()
    own = bb[0].astype(BF16).astype(F32)
    zs[...] = jnp.concatenate([own, jnp.zeros((64 - OWN, cfg.K), F32)], axis=0).astype(BF16)
    pl.semaphore_wait(barrier, len(peers))

    swap = rdma(zs, zr, zsem.at[0], zsem.at[1], partner)
    swap.start()
    swap.wait_recv()
    other = zr[...].astype(F32)[:OWN]
    unit = jnp.concatenate(
        [jnp.where(zl == 0, own, other), jnp.where(zl == 0, other, own)], axis=0
    ).astype(BF16)
    pos = lambda h: position(h, Y)
    ga[mx, 0] = unit[:A]
    gb[my, mx] = unit[A:]
    pending = [swap]
    xo = list(range(1, X))
    ta, tb = cfg.trees
    order = sorted(ta, key=pos)
    groups = [[0], [h for h in order if abs(h) <= 2], [h for h in order if abs(h) > 2]]
    groups = [h for h in groups if h]

    def below(t, h):
        return sorted([k for k, v in t.items() if v == h], key=lambda k: -abs(k))

    def send(src, dst, sems, i, device):
        cp = rdma(src, dst, sems.at[0, i], sems.at[1, i], device)
        cp.start()
        pending.append(cp)

    def arrived(dst, sems, i):
        rdma(dst, dst, sems.at[0, i], sems.at[1, i], partner).wait_recv()

    def flush():
        while pending:
            pending.pop().wait_send()

    def span(group):
        return pl.ds(pos(group[0]), len(group))

    def gather():
        ax, ay, bx, by = [gsem.at[i] for i in range(4)]
        for i, o in enumerate(xo):
            send(gb.at[my, mx], gb.at[my, mx], bx, i, dev(ox=o))

        def along_y_a(h):
            for k in below(ta, h):
                send(ga.at[mx, pos(h)], ga.at[mx, pos(k)], ay, pos(k), dev(oy=k - h))

        def along_x_a(n):
            part = ga.at[mx, span(groups[n])]
            for i, o in enumerate(xo):
                send(part, part, ax, n * X + i, dev(ox=o))

        def along_y_b(h):
            part = gb.at[(my - h + Y) % Y]
            for k in below(tb, h):
                send(part, part, by, pos(k), dev(oy=k - h))

        def wait_b(h):
            arrived(gb.at[(my - h + Y) % Y], by, pos(h))

        along_y_a(0)
        along_x_a(0)
        for i, o in enumerate(xo):
            arrived(gb.at[my, (mx - o + X) % X], bx, i)
        along_y_b(0)
        for h in sorted(groups[1], key=lambda h: -abs(h)):
            arrived(ga.at[mx, pos(h)], ay, pos(h))
            along_y_a(h)
        along_x_a(1)
        for h in sorted(groups[1], key=lambda h: -abs(h)):
            wait_b(h)
            along_y_b(h)
        for n in range(2, len(groups)):
            for h in groups[n]:
                arrived(ga.at[mx, pos(h)], ay, pos(h))
            along_x_a(n)
            for h in groups[n]:
                wait_b(h)
        for n in range(len(groups)):
            for i, o in enumerate(xo):
                arrived(ga.at[(mx - o + X) % X, span(groups[n])], ax, n * X + i)

    def arrange():
        def pair(i, carry):
            ux = i // (Y // 2)
            uy = (i % (Y // 2)) * 2
            a, b = [
                jnp.concatenate([ga[ux, pos(my - v + Y)].astype(F32), gb[v, ux].astype(F32)], axis=0)
                for v in (uy, uy + 1)
            ]
            for zz in range(ZL):
                rows = jnp.concatenate(
                    [a[zz * OWN:(zz + 1) * OWN], b[zz * OWN:(zz + 1) * OWN]], axis=0
                ).astype(BF16)
                at = pl.multiple_of(((zz * X + ux) * Y + uy) * OWN, 2 * OWN)
                q[pl.ds(at, 2 * OWN)] = rows
            return carry
        lax.fori_loop(0, X * Y // 2, pair, 0)

    TS = cfg.T // cfg.FE

    def sum_y():
        part = jnp.dot(xb[...], q[...], preferred_element_type=F32).astype(BF16)
        for h in range(C):
            for k in range(ZH):
                lo = (h * ZH + k) * TS
                ypart[h, k] = part[lo:lo + TS]
        mh = mz // ZL
        for h in range(1, C):
            cp = rdma(ypart.at[(mc + h) % C], ysib, y_sem.at[0, 0], y_sem.at[1, 0],
                      dev(oc=h))
            cp.start()
            pending.append(cp)
            cp.wait_recv()
        pair = ypart[mc].astype(F32) + ysib[...].astype(F32)
        ypair[...] = pair.astype(BF16)
        zoff = list(range(ZL, Z, ZL))
        for i, oz in enumerate(zoff):
            to = (mz + oz) % Z // ZL
            cp = rdma(ypair.at[to], yr.at[i], y_sem.at[0, 1 + i], y_sem.at[1, 1 + i],
                      dev(oz=oz))
            cp.start()
            pending.append(cp)
        flush()
        total = ypart[mc, mh].astype(F32) + ysib[mh].astype(F32)
        for i in range(len(zoff)):
            rdma(yr.at[i], yr.at[i], y_sem.at[0, 1 + i], y_sem.at[1, 1 + i],
                 partner).wait_recv()
            total = total + yr[i].astype(F32)
        yfull[mc, mh] = total.astype(BF16)
        slot = yfull.at[mc, mh]
        for i, oz in enumerate(zoff):
            cp = rdma(slot, slot, y_sem.at[2, 1 + i], y_sem.at[3, 1 + i], dev(oz=oz))
            cp.start()
            pending.append(cp)
        for i, oz in enumerate(zoff):
            slot = yfull.at[mc, (mz + Z - oz) % Z // ZL]
            rdma(slot, slot, y_sem.at[2, 1 + i], y_sem.at[3, 1 + i], partner).wait_recv()
        slot = yfull.at[mc]
        for h in range(1, C):
            cp = rdma(slot, slot, y_sem.at[2, 0], y_sem.at[3, 0], dev(oc=h))
            cp.start()
            pending.append(cp)
            slot = yfull.at[(mc + h) % C]
            rdma(slot, slot, y_sem.at[2, 0], y_sem.at[3, 0], dev(oc=h)).wait_recv()

    def product():
        y = yfull[...].reshape(cfg.T, cfg.K)
        zp[...] = lax.dot_general(xb[...], y, (((0,), (0,)), ((), ())), preferred_element_type=F32)

    def rows_a(hx, hy):
        u = ((mx - hx + X) % X) * Y + (my - hy + Y) % Y
        at0 = pl.multiple_of(u * OWN, OWN)
        at1 = pl.multiple_of((X * Y + u) * OWN, OWN)
        return jnp.concatenate([zp[pl.ds(at0, OWN)], zp[pl.ds(at1, A - OWN)]], axis=0)

    def rows_b(hx, hy):
        u = ((mx - hx + X) % X) * Y + (my - hy + Y) % Y
        return zp[pl.ds(pl.multiple_of((X * Y + u) * OWN + (A - OWN), 8), cfg.beta)]

    def scatter():
        ax, ay, bx, by = [ssem.at[i] for i in range(4)]
        def out_x_a(n):
            for i, o in enumerate(xo):
                for h in groups[n]:
                    sax[i, pos(h)] = rows_a(o, h).astype(BF16)
                part = span(groups[n])
                send(sax.at[i, part], rax.at[i, part], ax, n * X + i, dev(ox=-o))

        def out_y_b(h):
            for hx in range(X):
                v = rows_b(hx, h)
                for k in below(tb, h):
                    v = v + rby[pos(k), hx].astype(F32)
                sby[pos(h), hx] = v.astype(BF16)
            send(sby.at[pos(h)], rby.at[pos(h)], by, pos(h), dev(oy=tb[h] - h))

        def sum_a(h):
            v = rows_a(0, h)
            for i in range(len(xo)):
                v = v + rax[i, pos(h)].astype(F32)
            for k in below(ta, h):
                v = v + ray[pos(k)].astype(F32)
            return v

        def out_y_a(h):
            say[pos(h)] = sum_a(h).astype(BF16)
            send(say.at[pos(h)], ray.at[pos(h)], ay, pos(h), dev(oy=ta[h] - h))

        def wait_x_a(n):
            for i in range(len(xo)):
                arrived(rax.at[i, span(groups[n])], ax, n * X + i)

        def wait_y(buf, sems, t, h):
            for k in below(t, h):
                arrived(buf.at[pos(k)], sems, pos(k))

        far = [h for n in range(2, len(groups)) for h in groups[n]]
        mid = sorted(groups[1], key=lambda h: -abs(h))
        for h in far:
            out_y_b(h)
        for n in range(2, len(groups)):
            out_x_a(n)
        for h in mid:
            if not below(tb, h):
                out_y_b(h)
        out_x_a(1)
        out_x_a(0)
        for n in range(2, len(groups)):
            wait_x_a(n)
        for h in far:
            out_y_a(h)
        for h in mid:
            if below(tb, h):
                wait_y(rby, by, tb, h)
                out_y_b(h)
        wait_x_a(1)
        for h in mid:
            if not below(ta, h):
                out_y_a(h)
        for h in mid:
            if below(ta, h):
                wait_y(ray, ay, ta, h)
                out_y_a(h)
        wait_y(rby, by, tb, 0)
        for i, o in enumerate([0] + xo):
            v = rows_b(o, 0)
            for k in below(tb, 0):
                v = v + rby[pos(k), o].astype(F32)
            if o == 0:
                last_b = v
            else:
                sbx[i - 1] = v.astype(BF16)
                send(sbx.at[i - 1], rbx.at[i - 1], bx, i - 1, dev(ox=-o))
        wait_x_a(0)
        wait_y(ray, ay, ta, 0)
        fin[pl.ds(0, A)] = sum_a(0)
        for i in range(len(xo)):
            arrived(rbx.at[i], bx, i)
            last_b = last_b + rbx[i].astype(F32)
        fin[pl.ds(A, cfg.beta)] = last_b
        lo = fin[pl.ds(0, OWN)]
        hi = fin[pl.ds(OWN, OWN)]
        zx_s[...] = jnp.where(zl == 0, hi, lo)
        cp = rdma(zx_s, zx_r, zx_sem.at[0], zx_sem.at[1], partner)
        cp.start()
        pending.append(cp)
        flush()
        cp.wait_recv()
        return (jnp.where(zl == 0, lo, hi) + zx_r[...]) / float(cfg.TOTAL_T)

    def gram_sum(z):
        gl = lax.dot_general(z, z, (((0,), (0,)), ((), ())), precision=HI, preferred_element_type=F32)
        g1[0] = gl[:, :128]
        g1[1] = gl[:, 128:]
        RX, RZ = cfg.RX, cfg.RZ
        m = mc * X + mx

        def exchange(offs, sems, src, dst, wait):
            copies = []
            for i, off in enumerate(offs):
                cp = rdma(src(off), dst(i), sems.at[0, i], sems.at[1, i], dev(*off))
                cp.start()
                copies.append(cp)
            flush()
            for i, off in enumerate(offs):
                back = wait(i, off)
                rdma(back, back, sems.at[0, i], sems.at[1, i], dev(*off)).wait_recv()
            pending.extend(copies)

        xoff = [(ox, 0, 0, oc) for ox, oc in xc]
        zoff = [(0, 0, oz, 0) for oz in range(1, Z)]
        yoff = [(0, oy, 0, 0) for oy in range(1, Y)]

        def rows1(off):
            t = ((mc + off[3]) % C) * X + (mx + off[0] + X) % X
            return pl.ds(pl.multiple_of(t * RX, RX), RX)

        mine = pl.ds(pl.multiple_of(m * RX, RX), RX)
        exchange(xoff, m1, lambda off: g1.at[:, rows1(off)], lambda i: r1.at[i], lambda i, off: r1.at[i])
        total = g1[:, mine]
        for i in range(len(xoff)):
            total = total + r1[i]
        s1[...] = total

        def tile(z):
            return z % 2, pl.ds(pl.multiple_of((z // 2) * RZ, RZ), RZ)

        def tile_to(off):
            return tile((mz + off[2] + Z) % Z)

        exchange(zoff, m2, lambda off: s1.at[tile_to(off)], lambda i: r2.at[i], lambda i, off: r2.at[i])
        half, rows = tile(mz)
        total = s1[half, rows]
        for i in range(len(zoff)):
            total = total + r2[i]
        s2[...] = total
        exchange(yoff, m3, lambda off: s2, lambda i: r3.at[i], lambda i, off: r3.at[i])
        total = s2[...]
        for i in range(len(yoff)):
            total = total + r3[i]
        a2[half, rows] = total
        own_tile = a2.at[half, rows]
        exchange(zoff, m4, lambda off: own_tile, lambda i: own_tile,
                 lambda i, off: a2.at[tile((mz - off[2] + Z) % Z)])
        gfull[:, mine] = a2[...]
        near = [off for off in xoff if off[3] == 0]
        exchange(near, m5, lambda off: a2, lambda i: gfull.at[:, mine],
                 lambda i, off: gfull.at[:, rows1((-off[0], 0, 0, 0))])
        for h in range(1, C):
            def half(c):
                return gfull.at[:, pl.ds(pl.multiple_of(c % C * (X * RX), X * RX), X * RX)]
            cp = rdma(half(mc), half(mc), m5.at[0, len(near)], m5.at[1, len(near)], dev(oc=h))
            cp.start()
            pending.append(cp)
            rdma(half(mc + h), half(mc + h), m5.at[0, len(near)], m5.at[1, len(near)],
                 dev(oc=h)).wait_recv()
        gram_ref[...] = gfull[...]

    gather()
    load.wait()
    arrange()
    sum_y()
    product()
    z = scatter()
    z_ref[...] = z
    gram_sum(z)
    flush()


def communicate(cfg, basis, data, vmem=48 << 20):
    X, Y, Z, C, ZH = cfg.X, cfg.Y, cfg.Z, cfg.C, cfg.ZH
    K, OWN, T, FS, A, B = cfg.K, cfg.OWN, cfg.T, cfg.FS, cfg.alpha, cfg.beta
    TS = T // cfg.FE
    nx, nz, ny = cfg.MX - 1, Z - 1, Y - 1
    VM = pltpu.VMEM
    DMA = pltpu.SemaphoreType.DMA
    scratch = [
        VM((T, FS), BF16), VM((1, OWN, K), F32), VM((64, K), BF16), VM((64, K), BF16),
        VM((X, Y, A, K), BF16), VM((Y, X, B, K), BF16), VM((FS, K), BF16),
        VM((C, ZH, TS, K), BF16), VM((ZH, TS, K), BF16), VM((ZH, TS, K), BF16),
        VM((ZH, TS, K), BF16), VM((C, ZH, TS, K), BF16),
        VM((FS, K), F32), VM((X - 1, Y, A, K), BF16), VM((X - 1, Y, A, K), BF16),
        VM((Y, A, K), BF16), VM((Y, A, K), BF16), VM((Y, X, B, K), BF16), VM((Y, X, B, K), BF16),
        VM((X - 1, B, K), BF16), VM((X - 1, B, K), BF16),
        VM((2 * OWN, K), F32), VM((OWN, K), F32), VM((OWN, K), F32),
        VM((2, K, 128), F32), VM((nx, 2, cfg.RX, 128), F32), VM((2, cfg.RX, 128), F32),
        VM((nz, cfg.RZ, 128), F32), VM((cfg.RZ, 128), F32), VM((ny, cfg.RZ, 128), F32),
        VM((cfg.RZ, 128), F32), VM((2, cfg.RX, 128), F32), VM((2, K, 128), F32),
        DMA, DMA, DMA((2,)), DMA((4, 2, 3 * X + Y)), DMA((4, 1 + ZH)),
        DMA((4, 2, 3 * X + Y)), DMA((2,)),
        DMA((2, nx)), DMA((2, nz)), DMA((2, ny)), DMA((2, nz)), DMA((2, nx)),
    ]

    def body(*refs):
        comm_kernel(cfg, *refs)

    return pl.pallas_call(
        body,
        out_shape=(
            jax.ShapeDtypeStruct((OWN, K), F32),
            jax.ShapeDtypeStruct((2, K, 128), F32),
        ),
        in_specs=[pl.BlockSpec(memory_space=pltpu.HBM)] * 2,
        out_specs=(pl.BlockSpec(memory_space=pltpu.VMEM), pl.BlockSpec(memory_space=pltpu.VMEM)),
        scratch_shapes=scratch,
        compiler_params=pltpu.CompilerParams(
            collective_id=0, has_side_effects=True, vmem_limit_bytes=vmem
        ),
        name="power_step",
    )(
        pltpu.with_memory_space_constraint(basis, pltpu.HBM),
        pltpu.with_memory_space_constraint(data, pltpu.HBM),
    )


def split3(v):
    h = v.astype(BF16)
    r = v - h.astype(F32)
    m = r.astype(BF16)
    return h, m, (r - m.astype(F32)).astype(BF16)


def factor_kernel(scale, B, z_ref, gram_ref, out_ref, w):
    own, K = z_ref.shape
    w[:, 0:128] = gram_ref[0] * scale
    w[:, 128:256] = gram_ref[1] * scale
    w[:, 256:384] = jnp.concatenate([z_ref[...], jnp.zeros((128 - own, K), F32)], axis=0).T
    sub = lax.broadcasted_iota(jnp.int32, (8, 128), 0)
    G = B // 8
    for blk in range(K // B):
        r0 = blk * B
        t0 = r0 // 128
        tiles = list(range(t0, 3))
        v = [[w[r0 + 8 * s:r0 + 8 * s + 8, t * 128:(t + 1) * 128] for t in tiles] for s in range(G)]
        scales = []
        for s0 in range(G):
            lane = (r0 + 8 * s0) % 128
            col = {
                s: [jnp.broadcast_to(v[s][0][:, lane + k:lane + k + 1], (8, 128)) for k in range(8)]
                for s in range(s0, G)
            }
            dvec = jnp.zeros((8, 128), F32)
            for j in range(8):
                prow = [jnp.broadcast_to(v[s0][t][j:j + 1], (8, 128)) for t in range(len(tiles))]
                pcol = [jnp.broadcast_to(col[s0][k][j:j + 1], (8, 128)) if k >= j else None
                        for k in range(8)]
                inv = 1.0 / pcol[j]
                dvec = jnp.where(sub == j, pcol[j], dvec)
                for s in range(s0, G):
                    mult = col[s][j] * inv
                    if s == s0:
                        mult = jnp.where(sub > j, mult, 0.0)
                    for k in range(j + 1, 8):
                        col[s][k] = col[s][k] - mult * pcol[k]
                    for t in range(len(tiles)):
                        v[s][t] = v[s][t] - mult * prow[t]
            scales.append(lax.rsqrt(dvec))
        for s in range(G):
            for t in range(len(tiles)):
                v[s][t] = v[s][t] * scales[s]
                if tiles[t] == 2:
                    w[r0 + 8 * s:r0 + 8 * s + 8, 256:384] = v[s][t]
        if blk + 1 < K // B:
            rows = jnp.concatenate([jnp.concatenate(v[s], axis=1) for s in range(G)], axis=0)
            h, m, l = split3(rows)
            n0 = ((r0 + B) // 128) * 128 - t0 * 128
            left = jnp.concatenate([h, h, m, m, h, l], axis=0)
            right = jnp.concatenate([h, m, h, m, l, h], axis=0)
            upd = lax.dot_general(left[:, n0:K - t0 * 128], right[:, n0:], (((0,), (0,)), ((), ())),
                                  preferred_element_type=F32)
            c0 = t0 * 128 + n0
            w[r0 + B:K, c0:384] = w[r0 + B:K, c0:384] - upd[r0 + B - c0:]
    out_ref[0] = w[:, 256:384].T[:own]


def factor(cfg, z, gram, block=32):
    def body(z_ref, gram_ref, out_ref, w):
        factor_kernel(1.0 / float(cfg.F), block, z_ref, gram_ref, out_ref, w)

    return pl.pallas_call(
        body,
        out_shape=jax.ShapeDtypeStruct((1, cfg.OWN, cfg.K), F32),
        in_specs=[pl.BlockSpec(memory_space=pltpu.VMEM)] * 2,
        out_specs=pl.BlockSpec(memory_space=pltpu.VMEM),
        scratch_shapes=[pltpu.VMEM((cfg.K, 384), F32)],
        compiler_params=pltpu.CompilerParams(vmem_limit_bytes=8 << 20),
        name="factor_rows",
    )(z, gram)


def solution(mesh):
    cfg = Cfg(zl=2, x=4, y=8, zh=4, core=2, tokens=512)

    def per_device(data, basis):
        z, gram = communicate(cfg, basis, data)
        return factor(cfg, z, gram)

    return jax.shard_map(
        per_device, mesh=mesh, in_specs=(P("dp", "feat"), P("feat", "dp", None)),
        out_specs=P("feat", "dp", None), check_vma=False,
    )
```

time: 128 us -> 114 us (0.89)
  Pallas kernels: 123 us -> 114 us
  local copies, waits for them, and re-layouts: 4.15 us -> 0 us
    pallas_call x1, Pallas kernels: 114 us -> 106 us  [communicate(): pl.pallas_call(body, out_shape=(jax.ShapeDtypeStruct((OWN, K), F32), jax....]
    unnamed x8 -> x0, local copies, waits for them, and re-layouts: 4.15 us -> none
where the time goes in v2:
time: 114 us
  Pallas kernels  114 us (100%)
    pallas_call x1, Pallas kernels, communicate(): pl.pallas_call(body, out_shape=(jax.ShapeDtypeStruct((OWN, K), F32), jax....  106 us
    pallas_call x1, Pallas kernels, factor(): pl.pallas_call(body, out_shape=jax.ShapeDtypeStruct((1, cfg.OWN, cfg.K),...  8.34 us

profile of v2, /device:TPU:1, one launch (start us, length us, event | category | flops | bytes accessed | tf_op | source)
XLA Modules:
  0.0 114.3 jit_solution(15468210096334266215)
XLA Ops:
  0.0 106.0 %power_step.1 = (f32[56,256]{1,0:T(8,128)S(1)}, f32[2,256,128]{2,1,0:T(8,128)S(1)}) custom-call(f32[1,56,256]{2,1,0:T(8,128)} %refs_0_.1, bf16[512,3584]{1,0:T(8,128)(2,1)} %refs_1_.1), custom_call_target="tpu_custom_call" | custom-call | tf_op jit(solution)/shard_map/power_step/pallas_call | solution.py:452
  106.0 8.3 %factor_rows.1 = f32[1,56,256]{2,1,0:T(8,128)} custom-call(f32[56,256]{1,0:T(8,128)S(1)} %get-tuple-element.7.z_ref, f32[2,256,128]{2,1,0:T(8,128)S(1)} %get-tuple-element.8.gram_ref), custom_call_target="tpu_custom_call" | custom-call | tf_op jit(solution)/shard_map/factor_rows/pallas_call | solution.py:535

commit v3 on v2

--- a/solution.py
+++ b/solution.py
@@ -11,12 +11,17 @@
 HI = lax.Precision.HIGHEST
 
 
+TURN = 0.1
+LATER = 6
+
+
 class Cfg:
-    def __init__(self, zl, x, y, zh, core, tokens, own=56, width=256, alpha=80,
-                 trees=("skip", "skip")):
+    def __init__(self, zl, x, y, zh, core, tokens, own=56, width=256, alpha=80, chunks=1,
+                 trees=("skip", "skip", "skip", "skip")):
         self.ZL, self.X, self.Y, self.ZH, self.C = zl, x, y, zh, core
         self.T, self.OWN, self.K = tokens, own, width
         self.Z = zl * zh
+        self.NC, self.CW = chunks, width // chunks
         self.FE = zh * core
         self.DP = zl * x * y
         self.FS = own * self.DP
@@ -46,12 +51,15 @@
 
 
 def comm_kernel(cfg, basis_ref, data_hbm, z_ref, gram_ref,
-                xb, bb, zs, zr, ga, gb, q, ypart, ysib, ypair, yr, yfull, zp, sax, rax, say, ray, sby, rby, sbx, rbx, fin, zx_s, zx_r,
+                xb, bb, zs, zr, ga_all, gb_all, q_all, ypart_all, ysib_all, ypair_all, yr_all, yfull_all,
+                zp_all, sax_all, rax_all, say_all, ray_all, sby_all,
+                rby_all, sbx_all, rbx_all, fin_all, zx_s_all, zx_r_all, xt,
                 g1, r1, s1, r2, s2, r3, s3, a2, gfull,
-                xsem, bsem, zsem, gsem, y_sem, ssem, zx_sem,
+                xsem, bsem, zsem, gsem, y_sems, ssem, zx_sem,
                 m1, m2, m3, m4, m5):
     X, Y, Z, ZL, ZH, C = cfg.X, cfg.Y, cfg.Z, cfg.ZL, cfg.ZH, cfg.C
-    OWN, A = cfg.OWN, cfg.alpha
+    FS = cfg.FS
+    OWN, A, NC, CW = cfg.OWN, cfg.alpha, cfg.NC, cfg.CW
     dp = lax.axis_index("dp")
     feat = lax.axis_index("feat")
     my = dp % Y
@@ -103,14 +111,19 @@
         [jnp.where(zl == 0, own, other), jnp.where(zl == 0, other, own)], axis=0
     ).astype(BF16)
     pos = lambda h: position(h, Y)
-    ga[mx, 0] = unit[:A]
-    gb[my, mx] = unit[A:]
+    for c in range(NC):
+        ga_all[c, mx, 0] = unit[:A, c * CW:(c + 1) * CW]
+        gb_all[c, my, mx] = unit[A:, c * CW:(c + 1) * CW]
     pending = [swap]
     xo = list(range(1, X))
-    ta, tb = cfg.trees
+    ta, tb = cfg.trees[:2]
     order = sorted(ta, key=pos)
-    groups = [[0], [h for h in order if abs(h) <= 2], [h for h in order if abs(h) > 2]]
+    cuts = [(0, 0), (1, 1), (2, 2), (3, 3), (4, Y)]
+    groups = [[h for h in [0] + order if lo <= abs(h) <= hi] for lo, hi in cuts]
     groups = [h for h in groups if h]
+    first = [n for n in range(1, len(groups)) if abs(groups[n][0]) <= 2]
+    later = [n for n in range(1, len(groups)) if abs(groups[n][0]) > 2]
+    far = [h for n in later for h in groups[n]]
 
     def below(t, h):
         return sorted([k for k, v in t.items() if v == h], key=lambda k: -abs(k))
@@ -130,8 +143,10 @@
     def span(group):
         return pl.ds(pos(group[0]), len(group))
 
-    def gather():
-        ax, ay, bx, by = [gsem.at[i] for i in range(4)]
+    def gather(c):
+        ga, gb = ga_all.at[c], gb_all.at[c]
+        ax, ay, bx, by = [gsem.at[c, i] for i in range(4)]
+
         for i, o in enumerate(xo):
             send(gb.at[my, mx], gb.at[my, mx], bx, i, dev(ox=o))
 
@@ -154,27 +169,36 @@
 
         along_y_a(0)
         along_x_a(0)
+        yield 3.5
         for i, o in enumerate(xo):
             arrived(gb.at[my, (mx - o + X) % X], bx, i)
         along_y_b(0)
-        for h in sorted(groups[1], key=lambda h: -abs(h)):
-            arrived(ga.at[mx, pos(h)], ay, pos(h))
-            along_y_a(h)
-        along_x_a(1)
-        for h in sorted(groups[1], key=lambda h: -abs(h)):
-            wait_b(h)
-            along_y_b(h)
-        for n in range(2, len(groups)):
+        yield 4.5
+        for n in first:
+            for h in groups[n]:
+                arrived(ga.at[mx, pos(h)], ay, pos(h))
+                along_y_a(h)
+            along_x_a(n)
+        yield 8
+        for n in first[::-1]:
+            for h in groups[n]:
+                wait_b(h)
+                along_y_b(h)
+        yield 8.5
+        for n in later:
             for h in groups[n]:
                 arrived(ga.at[mx, pos(h)], ay, pos(h))
             along_x_a(n)
-            for h in groups[n]:
-                wait_b(h)
+        yield 12
+        for h in far:
+            wait_b(h)
         for n in range(len(groups)):
             for i, o in enumerate(xo):
                 arrived(ga.at[(mx - o + X) % X, span(groups[n])], ax, n * X + i)
 
-    def arrange():
+    def arrange(c):
+        ga, gb, q = ga_all.at[c], gb_all.at[c], q_all.at[c]
+
         def pair(i, carry):
             ux = i // (Y // 2)
             uy = (i % (Y // 2)) * 2
@@ -193,7 +217,9 @@
 
     TS = cfg.T // cfg.FE
 
-    def sum_y():
+    def sum_y(c):
+        ypart, ysib, ypair = ypart_all.at[c], ysib_all.at[c], ypair_all.at[c]
+        yr, yfull, q, y_sem = yr_all.at[c], yfull_all.at[c], q_all.at[c], y_sems.at[c]
         part = jnp.dot(xb[...], q[...], preferred_element_type=F32).astype(BF16)
         for h in range(C):
             for k in range(ZH):
@@ -205,6 +231,7 @@
                       dev(oc=h))
             cp.start()
             pending.append(cp)
+            yield 15
             cp.wait_recv()
         pair = ypart[mc].astype(F32) + ysib[...].astype(F32)
         ypair[...] = pair.astype(BF16)
@@ -215,7 +242,7 @@
                       dev(oz=oz))
             cp.start()
             pending.append(cp)
-        flush()
+        yield 20.5
         total = ypart[mc, mh].astype(F32) + ysib[mh].astype(F32)
         for i in range(len(zoff)):
             rdma(yr.at[i], yr.at[i], y_sem.at[0, 1 + i], y_sem.at[1, 1 + i],
@@ -227,6 +254,7 @@
             cp = rdma(slot, slot, y_sem.at[2, 1 + i], y_sem.at[3, 1 + i], dev(oz=oz))
             cp.start()
             pending.append(cp)
+        yield 26
         for i, oz in enumerate(zoff):
             slot = yfull.at[mc, (mz + Z - oz) % Z // ZL]
             rdma(slot, slot, y_sem.at[2, 1 + i], y_sem.at[3, 1 + i], partner).wait_recv()
@@ -235,25 +263,35 @@
             cp = rdma(slot, slot, y_sem.at[2, 0], y_sem.at[3, 0], dev(oc=h))
             cp.start()
             pending.append(cp)
+            yield 27.5
             slot = yfull.at[(mc + h) % C]
             rdma(slot, slot, y_sem.at[2, 0], y_sem.at[3, 0], dev(oc=h)).wait_recv()
 
-    def product():
-        y = yfull[...].reshape(cfg.T, cfg.K)
-        zp[...] = lax.dot_general(xb[...], y, (((0,), (0,)), ((), ())), preferred_element_type=F32)
-
-    def rows_a(hx, hy):
-        u = ((mx - hx + X) % X) * Y + (my - hy + Y) % Y
-        at0 = pl.multiple_of(u * OWN, OWN)
-        at1 = pl.multiple_of((X * Y + u) * OWN, OWN)
-        return jnp.concatenate([zp[pl.ds(at0, OWN)], zp[pl.ds(at1, A - OWN)]], axis=0)
-
-    def rows_b(hx, hy):
-        u = ((mx - hx + X) % X) * Y + (my - hy + Y) % Y
-        return zp[pl.ds(pl.multiple_of((X * Y + u) * OWN + (A - OWN), 8), cfg.beta)]
-
-    def scatter():
-        ax, ay, bx, by = [ssem.at[i] for i in range(4)]
+    def product(c):
+        y = yfull_all[c].reshape(cfg.T, CW)
+        zp_all[c] = jnp.dot(xt[...], y, preferred_element_type=F32)
+
+    def turn(n, of):
+        size = FS // of
+        xt[n * size:(n + 1) * size] = xb[:, n * size:(n + 1) * size].T
+
+    def scatter(c):
+        ta, tb = cfg.trees[2:]
+        zp, fin, zx_s, zx_r = zp_all.at[c], fin_all.at[c], zx_s_all.at[c], zx_r_all.at[c]
+        sax, rax, say, ray = sax_all.at[c], rax_all.at[c], say_all.at[c], ray_all.at[c]
+        sby, rby, sbx, rbx = sby_all.at[c], rby_all.at[c], sbx_all.at[c], rbx_all.at[c]
+        ax, ay, bx, by = [ssem.at[c, i] for i in range(4)]
+
+        def rows_a(hx, hy):
+            u = ((mx - hx + X) % X) * Y + (my - hy + Y) % Y
+            at0 = pl.multiple_of(u * OWN, OWN)
+            at1 = pl.multiple_of((X * Y + u) * OWN, OWN)
+            return jnp.concatenate([zp[pl.ds(at0, OWN)], zp[pl.ds(at1, A - OWN)]], axis=0)
+
+        def rows_b(hx, hy):
+            u = ((mx - hx + X) % X) * Y + (my - hy + Y) % Y
+            return zp[pl.ds(pl.multiple_of((X * Y + u) * OWN + (A - OWN), 8), cfg.beta)]
+
         def out_x_a(n):
             for i, o in enumerate(xo):
                 for h in groups[n]:
@@ -289,33 +327,35 @@
             for k in below(t, h):
                 arrived(buf.at[pos(k)], sems, pos(k))
 
-        far = [h for n in range(2, len(groups)) for h in groups[n]]
-        mid = sorted(groups[1], key=lambda h: -abs(h))
+        for n in later:
+            out_x_a(n)
         for h in far:
             out_y_b(h)
-        for n in range(2, len(groups)):
+        for n in first[::-1]:
             out_x_a(n)
-        for h in mid:
-            if not below(tb, h):
-                out_y_b(h)
-        out_x_a(1)
+            for h in groups[n]:
+                if not below(tb, h):
+                    out_y_b(h)
         out_x_a(0)
-        for n in range(2, len(groups)):
+        yield 34
+        for n in first[::-1]:
+            for h in groups[n]:
+                if below(tb, h):
+                    wait_y(rby, by, tb, h)
+                    out_y_b(h)
+        yield 35
+        for n in later:
             wait_x_a(n)
         for h in far:
             out_y_a(h)
-        for h in mid:
-            if below(tb, h):
-                wait_y(rby, by, tb, h)
-                out_y_b(h)
-        wait_x_a(1)
-        for h in mid:
-            if not below(ta, h):
+        yield 36
+        for n in first[::-1]:
+            wait_x_a(n)
+            for h in groups[n]:
+                if below(ta, h):
+                    wait_y(ray, ay, ta, h)
                 out_y_a(h)
-        for h in mid:
-            if below(ta, h):
-                wait_y(ray, ay, ta, h)
-                out_y_a(h)
+        yield 38.5
         wait_y(rby, by, tb, 0)
         for i, o in enumerate([0] + xo):
             v = rows_b(o, 0)
@@ -326,6 +366,7 @@
             else:
                 sbx[i - 1] = v.astype(BF16)
                 send(sbx.at[i - 1], rbx.at[i - 1], bx, i - 1, dev(ox=-o))
+        yield 41
         wait_x_a(0)
         wait_y(ray, ay, ta, 0)
         fin[pl.ds(0, A)] = sum_a(0)
@@ -336,12 +377,14 @@
         lo = fin[pl.ds(0, OWN)]
         hi = fin[pl.ds(OWN, OWN)]
         zx_s[...] = jnp.where(zl == 0, hi, lo)
-        cp = rdma(zx_s, zx_r, zx_sem.at[0], zx_sem.at[1], partner)
+        cp = rdma(zx_s, zx_r, zx_sem.at[c, 0], zx_sem.at[c, 1], partner)
         cp.start()
         pending.append(cp)
-        flush()
+        yield 45
         cp.wait_recv()
-        return (jnp.where(zl == 0, lo, hi) + zx_r[...]) / float(cfg.TOTAL_T)
+        z_ref[:, c * CW:(c + 1) * CW] = (
+            (jnp.where(zl == 0, lo, hi) + zx_r[...]) / float(cfg.TOTAL_T)
+        )
 
     def gram_sum(z):
         gl = lax.dot_general(z, z, (((0,), (0,)), ((), ())), precision=HI, preferred_element_type=F32)
@@ -411,38 +454,53 @@
                  dev(oc=h)).wait_recv()
         gram_ref[...] = gfull[...]
 
-    gather()
-    load.wait()
-    arrange()
-    sum_y()
-    product()
-    z = scatter()
-    z_ref[...] = z
-    gram_sum(z)
+    def chain(c):
+        yield from gather(c)
+        arrange(c)
+        yield from sum_y(c)
+        product(c)
+        yield from scatter(c)
+
+    def turns(of):
+        load.wait()
+        for n in range(of):
+            yield TURN + 0.5 * n
+            turn(n, of)
+
+    running = [[0.0, c, chain(c)] for c in range(NC)] + [[TURN, NC, turns(4)]]
+    while running:
+        running.sort(key=lambda r: r[:2])
+        step = running[0]
+        try:
+            step[0] = next(step[2]) + (LATER * step[1] if step[1] < NC else 0)
+        except StopIteration:
+            running.remove(step)
+    gram_sum(z_ref[...])
     flush()
 
 
 def communicate(cfg, basis, data, vmem=48 << 20):
     X, Y, Z, C, ZH = cfg.X, cfg.Y, cfg.Z, cfg.C, cfg.ZH
     K, OWN, T, FS, A, B = cfg.K, cfg.OWN, cfg.T, cfg.FS, cfg.alpha, cfg.beta
-    TS = T // cfg.FE
+    TS, N, W = T // cfg.FE, cfg.NC, cfg.CW
     nx, nz, ny = cfg.MX - 1, Z - 1, Y - 1
     VM = pltpu.VMEM
     DMA = pltpu.SemaphoreType.DMA
     scratch = [
         VM((T, FS), BF16), VM((1, OWN, K), F32), VM((64, K), BF16), VM((64, K), BF16),
-        VM((X, Y, A, K), BF16), VM((Y, X, B, K), BF16), VM((FS, K), BF16),
-        VM((C, ZH, TS, K), BF16), VM((ZH, TS, K), BF16), VM((ZH, TS, K), BF16),
-        VM((ZH, TS, K), BF16), VM((C, ZH, TS, K), BF16),
-        VM((FS, K), F32), VM((X - 1, Y, A, K), BF16), VM((X - 1, Y, A, K), BF16),
-        VM((Y, A, K), BF16), VM((Y, A, K), BF16), VM((Y, X, B, K), BF16), VM((Y, X, B, K), BF16),
-        VM((X - 1, B, K), BF16), VM((X - 1, B, K), BF16),
-        VM((2 * OWN, K), F32), VM((OWN, K), F32), VM((OWN, K), F32),
+        VM((N, X, Y, A, W), BF16), VM((N, Y, X, B, W), BF16), VM((N, FS, W), BF16),
+        VM((N, C, ZH, TS, W), BF16), VM((N, ZH, TS, W), BF16), VM((N, ZH, TS, W), BF16),
+        VM((N, ZH, TS, W), BF16), VM((N, C, ZH, TS, W), BF16),
+        VM((N, FS, W), F32), VM((N, X - 1, Y, A, W), BF16), VM((N, X - 1, Y, A, W), BF16),
+        VM((N, Y, A, W), BF16), VM((N, Y, A, W), BF16),
+        VM((N, Y, X, B, W), BF16), VM((N, Y, X, B, W), BF16),
+        VM((N, X - 1, B, W), BF16), VM((N, X - 1, B, W), BF16),
+        VM((N, 2 * OWN, W), F32), VM((N, OWN, W), F32), VM((N, OWN, W), F32), VM((FS, T), BF16),
         VM((2, K, 128), F32), VM((nx, 2, cfg.RX, 128), F32), VM((2, cfg.RX, 128), F32),
         VM((nz, cfg.RZ, 128), F32), VM((cfg.RZ, 128), F32), VM((ny, cfg.RZ, 128), F32),
         VM((cfg.RZ, 128), F32), VM((2, cfg.RX, 128), F32), VM((2, K, 128), F32),
-        DMA, DMA, DMA((2,)), DMA((4, 2, 3 * X + Y)), DMA((4, 1 + ZH)),
-        DMA((4, 2, 3 * X + Y)), DMA((2,)),
+        DMA, DMA, DMA((2,)), DMA((N, 4, 2, 5 * X)), DMA((N, 4, 1 + ZH)),
+        DMA((N, 4, 2, 5 * X)), DMA((N, 2)),
         DMA((2, nx)), DMA((2, nz)), DMA((2, ny)), DMA((2, nz)), DMA((2, nx)),
     ]
 

time: 114 us -> 114 us (level)
  no operation moved by 1% of the time
where the time goes in v3:
time: 114 us
  Pallas kernels  114 us (100%)
    pallas_call x1, Pallas kernels, communicate(): pl.pallas_call(body, out_shape=(jax.ShapeDtypeStruct((OWN, K), F32), jax....  105 us
    pallas_call x1, Pallas kernels, factor(): pl.pallas_call(body, out_shape=jax.ShapeDtypeStruct((1, cfg.OWN, cfg.K),...  8.34 us

profile of v3, /device:TPU:1, one launch (start us, length us, event | category | flops | bytes accessed | tf_op | source)
XLA Modules:
  0.0 113.7 jit_solution(17143100873511789605)
XLA Ops:
  0.0 105.3 %power_step.1 = (f32[56,256]{1,0:T(8,128)S(1)}, f32[2,256,128]{2,1,0:T(8,128)S(1)}) custom-call(f32[1,56,256]{2,1,0:T(8,128)} %refs_0_.1, bf16[512,3584]{1,0:T(8,128)(2,1)} %refs_1_.1), custom_call_target="tpu_custom_call" | custom-call | tf_op jit(solution)/shard_map/power_step/pallas_call | solution.py:510
  105.4 8.3 %factor_rows.1 = f32[1,56,256]{2,1,0:T(8,128)} custom-call(f32[56,256]{1,0:T(8,128)S(1)} %get-tuple-element.7.z_ref, f32[2,256,128]{2,1,0:T(8,128)S(1)} %get-tuple-element.8.gram_ref), custom_call_target="tpu_custom_call" | custom-call | tf_op jit(solution)/shard_map/factor_rows/pallas_call | solution.py:593

commit v4 on v3

--- a/solution.py
+++ b/solution.py
@@ -56,7 +56,7 @@
                 rby_all, sbx_all, rbx_all, fin_all, zx_s_all, zx_r_all, xt,
                 g1, r1, s1, r2, s2, r3, s3, a2, gfull,
                 xsem, bsem, zsem, gsem, y_sems, ssem, zx_sem,
-                m1, m2, m3, m4, m5):
+                m1, m2, m3, m4, m5, far_sem):
     X, Y, Z, ZL, ZH, C = cfg.X, cfg.Y, cfg.Z, cfg.ZL, cfg.ZH, cfg.C
     FS = cfg.FS
     OWN, A, NC, CW = cfg.OWN, cfg.alpha, cfg.NC, cfg.CW
@@ -90,21 +90,23 @@
     fetch = pltpu.make_async_copy(basis_ref, bb, bsem)
     fetch.start()
     xc = [(ox, oc) for ox in range(X) for oc in range(C) if (ox, oc) != (0, 0)]
-    fe = [(oz, oc) for oz in range(0, Z, ZL) for oc in range(C) if (oz, oc) != (0, 0)]
-    peers = {(0, 0, oz, oc) for oz, oc in fe}
-    peers |= {(ox, 0, 0, oc) for ox, oc in xc}
-    peers |= {(0, oy, 0, 0) for oy in range(1, Y)}
-    peers |= {(0, 0, oz, 0) for oz in range(1, Z)}
+    peers = {(o % X, 0, 0, 0) for o in range(1, X)}
+    peers |= {(0, o % Y, 0, 0) for o in (1, 2, -1, -2)}
+    peers |= {(0, 0, o % Z, 0) for o in (ZL, -ZL) if o % Z}
+    peers |= {(0, 0, 0, oc) for oc in range(1, C)}
     barrier = pltpu.get_barrier_semaphore()
+    pl.semaphore_signal(barrier, inc=1, device_id=partner, device_id_type=MESH)
     for peer in sorted(peers):
         pl.semaphore_signal(barrier, inc=1, device_id=dev(*peer), device_id_type=MESH)
     fetch.wait()
     own = bb[0].astype(BF16).astype(F32)
     zs[...] = jnp.concatenate([own, jnp.zeros((64 - OWN, cfg.K), F32)], axis=0).astype(BF16)
-    pl.semaphore_wait(barrier, len(peers))
+    pl.semaphore_wait(barrier, len(peers) + 1)
 
     swap = rdma(zs, zr, zsem.at[0], zsem.at[1], partner)
     swap.start()
+    if ZH > 1:
+        pl.semaphore_signal(far_sem, inc=1, device_id=dev(oz=ZL), device_id_type=MESH)
     swap.wait_recv()
     other = zr[...].astype(F32)[:OWN]
     unit = jnp.concatenate(
@@ -115,7 +117,8 @@
         ga_all[c, mx, 0] = unit[:A, c * CW:(c + 1) * CW]
         gb_all[c, my, mx] = unit[A:, c * CW:(c + 1) * CW]
     pending = [swap]
-    xo = list(range(1, X))
+    ring = lambda n: sorted(range(1, n), key=lambda o: -min(o, n - o))
+    xo = ring(X)
     ta, tb = cfg.trees[:2]
     order = sorted(ta, key=pos)
     cuts = [(0, 0), (1, 1), (2, 2), (3, 3), (4, Y)]
@@ -235,13 +238,16 @@
             cp.wait_recv()
         pair = ypart[mc].astype(F32) + ysib[...].astype(F32)
         ypair[...] = pair.astype(BF16)
-        zoff = list(range(ZL, Z, ZL))
+        zoff = [ZL * o for o in ring(ZH)]
+        if zoff:
+            pl.semaphore_wait(far_sem, 1)
         for i, oz in enumerate(zoff):
             to = (mz + oz) % Z // ZL
             cp = rdma(ypair.at[to], yr.at[i], y_sem.at[0, 1 + i], y_sem.at[1, 1 + i],
                       dev(oz=oz))
             cp.start()
             pending.append(cp)
+        flush()
         yield 20.5
         total = ypart[mc, mh].astype(F32) + ysib[mh].astype(F32)
         for i in range(len(zoff)):
@@ -269,11 +275,21 @@
 
     def product(c):
         y = yfull_all[c].reshape(cfg.T, CW)
-        zp_all[c] = jnp.dot(xt[...], y, preferred_element_type=F32)
+        tile = 2 * OWN * (4 if FS % (8 * OWN) == 0 else 1)
+
+        def one(i, carry):
+            rows = pl.ds(pl.multiple_of(i * tile, tile), tile)
+            zp_all[c, rows] = jnp.dot(xt[rows], y, preferred_element_type=F32)
+            return carry
+        lax.fori_loop(0, FS // tile, one, 0)
 
     def turn(n, of):
-        size = FS // of
-        xt[n * size:(n + 1) * size] = xb[:, n * size:(n + 1) * size].T
+        def one(i, carry):
+            rows = pl.ds(pl.multiple_of(i * 128, 128), 128)
+            xt[rows] = xb[:, rows].T
+            return carry
+        tiles = FS // 128
+        lax.fori_loop(n * tiles // of, (n + 1) * tiles // of, one, 0)
 
     def scatter(c):
         ta, tb = cfg.trees[2:]
@@ -376,14 +392,17 @@
         fin[pl.ds(A, cfg.beta)] = last_b
         lo = fin[pl.ds(0, OWN)]
         hi = fin[pl.ds(OWN, OWN)]
-        zx_s[...] = jnp.where(zl == 0, hi, lo)
+        zx_s[...] = jnp.concatenate(
+            [jnp.where(zl == 0, hi, lo), jnp.zeros((64 - OWN, CW), F32)], axis=0
+        ).astype(BF16)
         cp = rdma(zx_s, zx_r, zx_sem.at[c, 0], zx_sem.at[c, 1], partner)
         cp.start()
         pending.append(cp)
+        flush()
         yield 45
         cp.wait_recv()
         z_ref[:, c * CW:(c + 1) * CW] = (
-            (jnp.where(zl == 0, lo, hi) + zx_r[...]) / float(cfg.TOTAL_T)
+            (jnp.where(zl == 0, lo, hi) + zx_r[...].astype(F32)[:OWN]) / float(cfg.TOTAL_T)
         )
 
     def gram_sum(z):
@@ -400,14 +419,14 @@
                 cp.start()
                 copies.append(cp)
             flush()
-            for i, off in enumerate(offs):
+            for i, off in reversed(list(enumerate(offs))):
                 back = wait(i, off)
                 rdma(back, back, sems.at[0, i], sems.at[1, i], dev(*off)).wait_recv()
             pending.extend(copies)
 
-        xoff = [(ox, 0, 0, oc) for ox, oc in xc]
-        zoff = [(0, 0, oz, 0) for oz in range(1, Z)]
-        yoff = [(0, oy, 0, 0) for oy in range(1, Y)]
+        xoff = [(ox, 0, 0, oc) for ox in xo + [0] for oc in range(C) if (ox, oc) != (0, 0)]
+        zoff = [(0, 0, oz, 0) for oz in ring(Z)]
+        yoff = [(0, oy, 0, 0) for oy in ring(Y)]
 
         def rows1(off):
             t = ((mc + off[3]) % C) * X + (mx + off[0] + X) % X
@@ -495,13 +514,14 @@
         VM((N, Y, A, W), BF16), VM((N, Y, A, W), BF16),
         VM((N, Y, X, B, W), BF16), VM((N, Y, X, B, W), BF16),
         VM((N, X - 1, B, W), BF16), VM((N, X - 1, B, W), BF16),
-        VM((N, 2 * OWN, W), F32), VM((N, OWN, W), F32), VM((N, OWN, W), F32), VM((FS, T), BF16),
+        VM((N, 2 * OWN, W), F32), VM((N, 64, W), BF16), VM((N, 64, W), BF16), VM((FS, T), BF16),
         VM((2, K, 128), F32), VM((nx, 2, cfg.RX, 128), F32), VM((2, cfg.RX, 128), F32),
         VM((nz, cfg.RZ, 128), F32), VM((cfg.RZ, 128), F32), VM((ny, cfg.RZ, 128), F32),
         VM((cfg.RZ, 128), F32), VM((2, cfg.RX, 128), F32), VM((2, K, 128), F32),
         DMA, DMA, DMA((2,)), DMA((N, 4, 2, 5 * X)), DMA((N, 4, 1 + ZH)),
         DMA((N, 4, 2, 5 * X)), DMA((N, 2)),
         DMA((2, nx)), DMA((2, nz)), DMA((2, ny)), DMA((2, nz)), DMA((2, nx)),
+        pltpu.SemaphoreType.REGULAR,
     ]
 
     def body(*refs):

time: 114 us -> 111 us (0.974)
  Pallas kernels: 114 us -> 111 us
    pallas_call x1, Pallas kernels: 105 us -> 103 us  [communicate(): pl.pallas_call(body, out_shape=(jax.ShapeDtypeStruct((OWN, K), F32), jax....]
where the time goes in v4:
time: 111 us
  Pallas kernels  111 us (100%)
    pallas_call x1, Pallas kernels, communicate(): pl.pallas_call(body, out_shape=(jax.ShapeDtypeStruct((OWN, K), F32), jax....  103 us
    pallas_call x1, Pallas kernels, factor(): pl.pallas_call(body, out_shape=jax.ShapeDtypeStruct((1, cfg.OWN, cfg.K),...  8.34 us

profile of v4, /device:TPU:1, one launch (start us, length us, event | category | flops | bytes accessed | tf_op | source)
XLA Modules:
  0.0 110.9 jit_solution(2697571791812613310)
XLA Ops:
  0.0 102.5 %power_step.1 = (f32[56,256]{1,0:T(8,128)S(1)}, f32[2,256,128]{2,1,0:T(8,128)S(1)}) custom-call(f32[1,56,256]{2,1,0:T(8,128)} %refs_0_.1, bf16[512,3584]{1,0:T(8,128)(2,1)} %refs_1_.1), custom_call_target="tpu_custom_call" | custom-call | tf_op jit(solution)/shard_map/power_step/pallas_call | solution.py:530
  102.5 8.3 %factor_rows.1 = f32[1,56,256]{2,1,0:T(8,128)} custom-call(f32[56,256]{1,0:T(8,128)S(1)} %get-tuple-element.7.z_ref, f32[2,256,128]{2,1,0:T(8,128)S(1)} %get-tuple-element.8.gram_ref), custom_call_target="tpu_custom_call" | custom-call | tf_op jit(solution)/shard_map/factor_rows/pallas_call | solution.py:613

commit v5 on v4

--- a/solution.py
+++ b/solution.py
@@ -150,9 +150,6 @@
         ga, gb = ga_all.at[c], gb_all.at[c]
         ax, ay, bx, by = [gsem.at[c, i] for i in range(4)]
 
-        for i, o in enumerate(xo):
-            send(gb.at[my, mx], gb.at[my, mx], bx, i, dev(ox=o))
-
         def along_y_a(h):
             for k in below(ta, h):
                 send(ga.at[mx, pos(h)], ga.at[mx, pos(k)], ay, pos(k), dev(oy=k - h))
@@ -160,7 +157,23 @@
         def along_x_a(n):
             part = ga.at[mx, span(groups[n])]
             for i, o in enumerate(xo):
+                if n in relayed and o == X // 2:
+                    continue
                 send(part, part, ax, n * X + i, dev(ox=o))
+
+        relayed = [n for n in (0, 1) if X == 4 and n in [0] + first]
+        went = set()
+
+        def wait_x_a(n, o):
+            if (n, o) not in went:
+                arrived(ga.at[(mx - o + X) % X, span(groups[n])], ax, n * X + xo.index(o))
+                went.add((n, o))
+
+        def relay(n):
+            o = 1 if n % 2 == 0 else X - 1
+            wait_x_a(n, o)
+            part = ga.at[(mx - o + X) % X, span(groups[n])]
+            send(part, part, ax, n * X + xo.index(X // 2), dev(ox=o))
 
         def along_y_b(h):
             part = gb.at[(my - h + Y) % Y]
@@ -171,6 +184,8 @@
             arrived(gb.at[(my - h + Y) % Y], by, pos(h))
 
         along_y_a(0)
+        for i, o in enumerate(xo):
+            send(gb.at[my, mx], gb.at[my, mx], bx, i, dev(ox=o))
         along_x_a(0)
         yield 3.5
         for i, o in enumerate(xo):
@@ -187,6 +202,8 @@
             for h in groups[n]:
                 wait_b(h)
                 along_y_b(h)
+        for n in relayed:
+            relay(n)
         yield 8.5
         for n in later:
             for h in groups[n]:
@@ -196,8 +213,8 @@
         for h in far:
             wait_b(h)
         for n in range(len(groups)):
-            for i, o in enumerate(xo):
-                arrived(ga.at[(mx - o + X) % X, span(groups[n])], ax, n * X + i)
+            for o in xo:
+                wait_x_a(n, o)
 
     def arrange(c):
         ga, gb, q = ga_all.at[c], gb_all.at[c], q_all.at[c]
@@ -406,7 +423,11 @@
         )
 
     def gram_sum(z):
-        gl = lax.dot_general(z, z, (((0,), (0,)), ((), ())), precision=HI, preferred_element_type=F32)
+        h, m, l = split3(jnp.concatenate([z, jnp.zeros((64 - OWN, cfg.K), F32)], axis=0))
+        gl = lax.dot_general(
+            jnp.concatenate([h, h, m, m, h, l], axis=0), jnp.concatenate([h, m, h, m, l, h], axis=0),
+            (((0,), (0,)), ((), ())), preferred_element_type=F32,
+        )
         g1[0] = gl[:, :128]
         g1[1] = gl[:, 128:]
         RX, RZ = cfg.RX, cfg.RZ

time: 111 us -> 111 us (level)
  no operation moved by 1% of the time
where the time goes in v5:
time: 111 us
  Pallas kernels  111 us (100%)
    pallas_call x1, Pallas kernels, communicate(): pl.pallas_call(body, out_shape=(jax.ShapeDtypeStruct((OWN, K), F32), jax....  102 us
    pallas_call x1, Pallas kernels, factor(): pl.pallas_call(body, out_shape=jax.ShapeDtypeStruct((1, cfg.OWN, cfg.K),...  8.34 us

profile of v5, /device:TPU:1, one launch (start us, length us, event | category | flops | bytes accessed | tf_op | source)
XLA Modules:
  0.0 110.6 jit_solution(12527753077504567239)
XLA Ops:
  0.0 102.2 %power_step.1 = (f32[56,256]{1,0:T(8,128)S(1)}, f32[2,256,128]{2,1,0:T(8,128)S(1)}) custom-call(f32[1,56,256]{2,1,0:T(8,128)} %refs_0_.1, bf16[512,3584]{1,0:T(8,128)(2,1)} %refs_1_.1), custom_call_target="tpu_custom_call" | custom-call | tf_op jit(solution)/shard_map/power_step/pallas_call | solution.py:551
  102.2 8.3 %factor_rows.1 = f32[1,56,256]{2,1,0:T(8,128)} custom-call(f32[56,256]{1,0:T(8,128)S(1)} %get-tuple-element.7.z_ref, f32[2,256,128]{2,1,0:T(8,128)S(1)} %get-tuple-element.8.gram_ref), custom_call_target="tpu_custom_call" | custom-call | tf_op jit(solution)/shard_map/factor_rows/pallas_call | solution.py:634

commit v6 on v5

--- a/solution.py
+++ b/solution.py
@@ -17,7 +17,7 @@
 
 class Cfg:
     def __init__(self, zl, x, y, zh, core, tokens, own=56, width=256, alpha=80, chunks=1,
-                 trees=("skip", "skip", "skip", "skip")):
+                 trees=("skip", "skip", "direct", "skip")):
         self.ZL, self.X, self.Y, self.ZH, self.C = zl, x, y, zh, core
         self.T, self.OWN, self.K = tokens, own, width
         self.Z = zl * zh

time: 111 us -> 110 us (level)
  no operation moved by 1% of the time
where the time goes in v6:
time: 110 us
  Pallas kernels  110 us (100%)
    pallas_call x1, Pallas kernels, communicate(): pl.pallas_call(body, out_shape=(jax.ShapeDtypeStruct((OWN, K), F32), jax....  102 us
    pallas_call x1, Pallas kernels, factor(): pl.pallas_call(body, out_shape=jax.ShapeDtypeStruct((1, cfg.OWN, cfg.K),...  8.34 us

profile of v6, /device:TPU:1, one launch (start us, length us, event | category | flops | bytes accessed | tf_op | source)
XLA Modules:
  0.0 110.3 jit_solution(7165393939038734340)
XLA Ops:
  0.0 102.0 %power_step.1 = (f32[56,256]{1,0:T(8,128)S(1)}, f32[2,256,128]{2,1,0:T(8,128)S(1)}) custom-call(f32[1,56,256]{2,1,0:T(8,128)} %refs_0_.1, bf16[512,3584]{1,0:T(8,128)(2,1)} %refs_1_.1), custom_call_target="tpu_custom_call" | custom-call | tf_op jit(solution)/shard_map/power_step/pallas_call | solution.py:551
  102.0 8.3 %factor_rows.1 = f32[1,56,256]{2,1,0:T(8,128)} custom-call(f32[56,256]{1,0:T(8,128)S(1)} %get-tuple-element.7.z_ref, f32[2,256,128]{2,1,0:T(8,128)S(1)} %get-tuple-element.8.gram_ref), custom_call_target="tpu_custom_call" | custom-call | tf_op jit(solution)/shard_map/factor_rows/pallas_call | solution.py:634
